TPU v7x, 32 devices: a whole 2x2x4 slice. The times are simulated.
32 devices in a mesh: groups: 2 (over x), dev: 16 (over z, y, core).
Axes of the slice: x: 2, y: 2, z: 4, core: 2. Of those that a mesh axis runs over, the one named last changes fastest.
Arguments:
- queries: bfloat16 [1024, 4096], P(('groups', 'dev')), parts along dimension 0, may hold values from -6 to 6
- keys: bfloat16 [1024, 160, 256], P(('groups', 'dev')), parts along dimension 0, may hold values from -6 to 6
- values: bfloat16 [1024, 160, 256], P(('groups', 'dev')), parts along dimension 0, may hold values from -6 to 6
- lengths: int32 [1024], P(('groups', 'dev')), parts along dimension 0, may hold values from 2 to 160, as said below
- residual: bfloat16 [1024, 4096], P(('groups', 'dev')), parts along dimension 0, may hold values from -36 to 36
- out_weight: bfloat16 [4096, 4096], P(None, 'dev'), may hold values from -0.09375 to 0.09375
- norm_gain: bfloat16 [4096], replicated, may hold values from 0.099609375 to 1.8984375
- expert_ids: int32 [1024, 8], P(('groups', 'dev')), parts along dimension 0, may hold values from 0 to 15, all different within a row; in each aligned block of 32 rows (0 to 31, 32 to 63, ...) at most 32 rows name the same one
- routed_gate_weight: float32 [1024, 8], P(('groups', 'dev')), parts along dimension 0, may hold values from 0.05 to 0.5
- w_gate: bfloat16 [16, 4096, 768], P('dev'), may hold values from -0.09375 to 0.09375
- w_up: bfloat16 [16, 4096, 768], P('dev'), may hold values from -0.09375 to 0.09375
- w_down: bfloat16 [16, 768, 4096], P('dev'), may hold values from -0.21875 to 0.21875
Outputs:
- layer_out: bfloat16 [1024, 4096], P(('groups', 'dev')), parts along dimension 0
There are 2 independent parts, one for each index of `groups`. A program takes and returns all parts, laid end to end along the dimension named above; an argument that names none is the same for every part. Nothing has to cross between parts.
Inputs may be any that keep to these rules, and one draw needn't show every extreme that they name: `lengths`: some sequence has 160 live positions. `expert_ids`: each token names 8 different experts; among the 32 tokens of one index of dev (aligned blocks of rows) no expert is named more than 32 times, a bound that some block reaches.
All inputs are finite; a program needn't handle non-finite values.
Results may differ from a plain program's by a relative error of at most 0.006.
Values may be sent and summed in bfloat16 or wider, within the bound.
A program may use at most 128 MiB of HBM per device.

v0:
```python
import math

import jax
import jax.numpy as jnp
from jax import lax
from jax.sharding import PartitionSpec as P

HQ = 32
KVH = 2
HD = 128


def attend(queries, keys, values, lengths):
    seq_rows = queries.shape[0]
    token_position_index = keys.shape[1]
    query_heads = queries.reshape(seq_rows, KVH, HQ // KVH, HD)
    key_heads = keys.reshape(seq_rows, token_position_index, KVH, HD)
    value_heads = values.reshape(seq_rows, token_position_index, KVH, HD)
    scores = jnp.einsum(
        "bgqd,bpgd->bgqp", query_heads, key_heads, preferred_element_type=jnp.float32
    ) * (1.0 / math.sqrt(HD))
    live = (
        jnp.arange(token_position_index, dtype=jnp.int32)[None, None, None, :]
        < lengths[:, None, None, None]
    )
    scores = jnp.where(live, scores, jnp.float32(-1e30))
    highest = jnp.max(scores, axis=-1, keepdims=True)
    weights = jnp.exp(scores - highest)
    probs = (weights / jnp.sum(weights, axis=-1, keepdims=True)).astype(jnp.bfloat16)
    mixed = jnp.einsum("bgqp,bpgd->bgqd", probs, value_heads, preferred_element_type=jnp.float32)
    return mixed.reshape(seq_rows, HQ * HD).astype(jnp.bfloat16)


def expert_rows(row_block, w_gate, w_up, w_down):
    gate_part = jnp.dot(row_block, w_gate[0], preferred_element_type=jnp.float32)
    up_part = jnp.dot(row_block, w_up[0], preferred_element_type=jnp.float32)
    inner = (jax.nn.silu(gate_part) * up_part).astype(jnp.bfloat16)
    return jnp.dot(inner, w_down[0], preferred_element_type=jnp.float32).astype(jnp.bfloat16)


def per_device(
    queries,
    keys,
    values,
    lengths,
    residual,
    out_weight,
    norm_gain,
    expert_ids,
    routed_gate_weight,
    w_gate,
    w_up,
    w_down,
):
    seq_rows = queries.shape[0]
    attended = attend(queries, keys, values, lengths)
    projected = jnp.dot(
        attended,
        lax.all_gather(out_weight, "dev", axis=1, tiled=True),
        preferred_element_type=jnp.float32,
    ).astype(jnp.bfloat16)
    stream = residual.astype(jnp.float32) + projected.astype(jnp.float32)
    scale = lax.rsqrt(jnp.mean(stream * stream, axis=-1, keepdims=True) + 1e-06)
    normalized_input = (stream * scale * norm_gain.astype(jnp.float32)).astype(jnp.bfloat16)
    model_width = normalized_input.shape[1]
    expert_count = lax.axis_size("dev")
    selected_expert_count = expert_ids.shape[1]
    capacity = 2 * seq_rows * selected_expert_count // expert_count
    flattened_expert_index = expert_ids.reshape(-1)
    one_hot = (
        flattened_expert_index[:, None] == jnp.arange(expert_count, dtype=jnp.int32)[None, :]
    ).astype(jnp.int32)
    earlier = jnp.cumsum(one_hot, axis=0) - one_hot
    slot_index = jnp.sum(earlier * one_hot, axis=1)
    target = flattened_expert_index * capacity + slot_index
    source_row = (
        jnp.arange(seq_rows * selected_expert_count, dtype=jnp.int32) // selected_expert_count
    )
    packed = (
        jnp.zeros((expert_count * capacity, model_width), jnp.bfloat16)
        .at[target]
        .set(normalized_input[source_row])
    )
    packed = packed.reshape(expert_count, capacity, model_width)
    block = lax.all_to_all(packed, "dev", split_axis=0, concat_axis=0, tiled=True)
    senders, slot_count, width = block.shape
    result = expert_rows(block.reshape(senders * slot_count, width), w_gate, w_up, w_down)
    result = result.reshape(senders, slot_count, width)
    returned = lax.all_to_all(result, "dev", split_axis=0, concat_axis=0, tiled=True)
    selected_experts = returned.reshape(expert_count * capacity, model_width)[target]
    selected_experts = selected_experts.reshape(
        seq_rows, selected_expert_count, model_width
    ).astype(jnp.float32)
    mixed_expert_output = jnp.einsum("cz,czw->cw", routed_gate_weight, selected_experts)
    return (stream + mixed_expert_output).astype(jnp.bfloat16)


def solution(mesh):
    in_specs = (
        P(("groups", "dev"), None),
        P(("groups", "dev"), None, None),
        P(("groups", "dev"), None, None),
        P(("groups", "dev")),
        P(("groups", "dev"), None),
        P(None, "dev"),
        P(),
        P(("groups", "dev"), None),
        P(("groups", "dev"), None),
        P("dev", None, None),
        P("dev", None, None),
        P("dev", None, None),
    )
    out_specs = P(("groups", "dev"), None)
    return jax.shard_map(
        per_device, mesh=mesh, in_specs=in_specs, out_specs=out_specs, check_vma=False
    )
```

profile of v0, /device:TPU:13, one launch (start us, length us, event | category | flops | bytes accessed | tf_op | source)
XLA Modules:
  0.0 449.7 jit_solution(17079764456606303071)
XLA Ops:
  6.5 0.0 copy-start
  6.5 0.0 copy-start.4
  6.5 0.0 copy-start.5
  6.5 0.0 copy-start.7
  6.5 0.0 all-gather.2.cloned.1.call-start
  6.6 0.7 all-gather.2.cloned.1.call-update
  7.3 0.8 copy.18
  8.1 0.1 eq.29
  8.2 0.1 eq.25
  8.3 1.0 copy.26
  9.3 0.0 copy-done.5
  9.3 0.6 reduce-window.6
  9.9 0.2 slice_reduce_fusion
  10.1 0.0 copy-done.4
  10.1 0.1 copy.17
  10.2 0.1 mul.51
  10.3 0.1 fusion.44
  10.4 0.0 copy-done.7
  10.4 0.1 iota_compare_fusion
  10.5 0.0 copy-done
  10.5 2.6 fusion.47
  13.1 0.0 copy-start.3
  13.1 2.9 fusion.33
  16.0 171.1 %all-gather.2.cloned.1.call-done = bf16[4096,4096]{1,0:T(8,128)(2,1)} async-done(((bf16[4096,256]{1,0:T(8,128)(2,1)}), bf16[4096,4096]{1,0:T(8,128)(2,1)}) %all-gather.2.cloned.1.call-update) | async-done | bytes 33554448 | tf_op jit(solution)/shard_map/all_gather | solution.py:59
  187.2 0.0 copy-done.3
  187.2 13.7 %multiply_reduce_fusion = (f32[32]{0:T(128)S(1)}, f32[32,4096]{1,0:T(8,128)S(1)}) fusion(bf16[4096,4096]{1,0:T(8,128)(2,1)} %all-gather.2.cloned.1.call-done, bf16[4,8,32,128]{3,2,1,0:T(8,128)(2,1)S(1)} %bitcast.91, bf16[32,4096]{1,0:T(8,128)(2,1)S(1)} %copy-done.3), kind=kOutput, calls=%fused_computation.35 | convolution fusion | flops 1074528256 | bytes 34603136 | tf_op jit(solution)/shard_map/dot_general | solution.py:57
  200.9 0.1 multiply_convert_fusion.1
  201.0 12.3 %scatter_custom_fusion = bf16[512,4096]{1,0:T(8,128)(2,1)} fusion(s32[256]{0:T(256)S(1)} %bitcast.95, bf16[32,4096]{1,0:T(8,128)(2,1)S(1)} %multiply_convert_fusion.1, s32[1024]{0:T(1024)S(1)} %pad_clamp_fusion.1, bf16[]{:T(256)} %constant.35.clone.1), kind=kCustom, calls=%fused_computation.22 | custom fusion | bytes 4194306 | tf_op jit(solution)/shard_map/scatter | solution.py:82
  213.3 96.5 %all_to_all.10 = bf16[16,32,4096]{2,1,0:T(8,128)(2,1)S(1)} all-to-all(bf16[16,32,4096]{2,1,0:T(8,128)(2,1)} %bitcast.87), channel_id=1, replica_groups=mesh['groups'=2,'dev'=16] {'dev'}, dimensions={0} | all-to-all | bytes 8388608 | tf_op jit(solution)/shard_map/all_to_all | solution.py:85
  309.8 0.0 copy-start.2
  309.8 1.9 copy-done.2
  311.7 5.5 %fusion.5 = f32[512,768]{1,0:T(8,128)S(1)} fusion(bf16[512,4096]{1,0:T(8,128)(2,1)S(1)} %bitcast.89, bf16[1,4096,768]{2,1,0:T(8,128)(2,1)} %param.21), kind=kOutput, calls=%fused_computation.8 | convolution fusion | flops 3221225472 | bytes 12058624 | tf_op jit(solution)/shard_map/dot_general | solution.py:35
  317.3 16.6 %fusion.7 = bf16[512,4096]{1,0:T(8,128)(2,1)} fusion(bf16[1,768,4096]{2,1,0:T(8,128)(2,1)} %param.23, f32[512,768]{1,0:T(8,128)S(1)} %fusion.5, bf16[512,4096]{1,0:T(8,128)(2,1)} %bitcast.90, bf16[1,4096,768]{2,1,0:T(8,128)(2,1)} %param.22), kind=kOutput, calls=%fused_computation.10 | convolution fusion | flops 6446907392 | bytes 22544384 | tf_op jit(solution)/shard_map/dot_general | solution.py:38
  333.8 0.0 copy-start.6
  333.8 5.2 %all-to-all-start.1 = ((bf16[16,32,4096]{2,1,0:T(8,128)(2,1)}), bf16[16,32,4096]{2,1,0:T(8,128)(2,1)}, u32[]{:S(2)}, u32[]{:S(2)}) async-start(bf16[16,32,4096]{2,1,0:T(8,128)(2,1)} %bitcast.88), calls=%async_computation.1 | async-start | bytes 8388608 | tf_op jit(solution)/shard_map/all_to_all | solution.py:89
  339.0 0.0 copy-done.6
  339.0 0.1 copy.21
  339.1 92.4 %all-to-all-done.1 = bf16[16,32,4096]{2,1,0:T(8,128)(2,1)} async-done(((bf16[16,32,4096]{2,1,0:T(8,128)(2,1)}), bf16[16,32,4096]{2,1,0:T(8,128)(2,1)}, u32[]{:S(2)}, u32[]{:S(2)}) %all-to-all-start.1) | async-done | bytes 4194336 | tf_op jit(solution)/shard_map/all_to_all | solution.py:89
  431.5 0.0 copy-start.1
  431.5 8.1 %gather_fusion = bf16[256,4096]{1,0:T(8,128)(2,1)} fusion(bf16[512,4096]{1,0:T(8,128)(2,1)} %bitcast.10, s32[1024]{0:T(1024)S(1)} %pad_clamp_fusion), kind=kCustom, calls=%fused_computation.1 | custom fusion | bytes 4195328 | tf_op jit(solution)/shard_map/gather | solution.py:90
  439.6 2.3 fusion.18
  441.8 1.0 fusion.38
  442.9 0.0 copy-done.1
  (10 shorter events, 0.1 us)
Async XLA Ops:
  6.5 4.0 copy-start
  6.5 3.6 copy-start.4
  6.5 2.7 copy-start.5
  6.5 3.9 copy-start.7
  6.5 180.6 %all-gather.2.cloned.1.call-start = ((), (), s32[]{:S(2)}) async-start(), calls=%async_computation.2 | async-start | bytes 35651584 | tf_op jit(solution)/shard_map/all_gather | solution.py:59
  13.1 174.1 %copy-start.3 = (bf16[32,4096]{1,0:T(8,128)(2,1)S(1)}, bf16[32,4096]{1,0:T(8,128)(2,1)}, u32[]{:S(2)}) copy-start(bf16[32,4096]{1,0:T(8,128)(2,1)} %param.16) | copy-start | bytes 786436
  309.8 1.9 copy-start.2
  333.8 5.2 %copy-start.6 = (f32[32,8]{0,1:T(8,128)S(1)}, f32[32,8]{0,1:T(8,128)}, u32[]{:S(2)}) copy-start(f32[32,8]{0,1:T(8,128)} %param.20) | copy-start | bytes 3076
  333.8 97.6 %all-to-all-start.1 = ((bf16[16,32,4096]{2,1,0:T(8,128)(2,1)}), bf16[16,32,4096]{2,1,0:T(8,128)(2,1)}, u32[]{:S(2)}, u32[]{:S(2)}) async-start(bf16[16,32,4096]{2,1,0:T(8,128)(2,1)} %bitcast.88), calls=%async_computation.1 | async-start | bytes 8388608 | tf_op jit(solution)/shard_map/all_to_all | solution.py:89
  431.5 11.4 %copy-start.1 = (bf16[32,160,256]{2,1,0:T(8,128)(2,1)S(1)}, bf16[32,160,256]{2,1,0:T(8,128)(2,1)}, u32[]{:S(2)}) copy-start(bf16[32,160,256]{2,1,0:T(8,128)(2,1)} %param.13) | copy-start | bytes 7864324
Sparse Core Ops, SparseCore 0:
  8.9 178.2 all-gather.1
where the time goes:
time: 450 us
  waiting for transfers between devices  264 us (59%)
  blocking collectives  96.5 us (21%)
  matrix products  43.6 us (10%)
  local copies, waits for them, and re-layouts  24.7 us (5%)
  between operations  13.5 us (3%)
  starting transfers between devices  5.2 us (1%)
    all_gather x1, waiting for transfers between devices, per_device(): lax.all_gather(out_weight, 'dev', axis=1, tiled=True)  171 us
    all_to_all x1, blocking collectives, per_device(): lax.all_to_all(packed, 'dev', split_axis=0, concat_axis=0, tiled=True)  96.5 us
    all_to_all x1, waiting for transfers between devices, per_device(): lax.all_to_all(result, 'dev', split_axis=0, concat_axis=0, tiled=True)  92.4 us
    dot_general x1, matrix products, expert_rows(): jnp.dot(inner, w_down[0], preferred_element_type=jnp.float32)  16.6 us
    dot_general x1, matrix products, per_device(): jnp.dot(attended, lax.all_gather(out_weight, 'dev', axis=1, tiled=True),...  13.7 us
    scatter x1, local copies, waits for them, and re-layouts, per_device(): packed = jnp.zeros((expert_count * capacity, model_width), jnp.bfloat16)....  12.3 us
  transfers between devices with their start and end apart: 2, of which 2 were waited for; matrix products, arithmetic and copies ran while one was open for 2% of the time, Pallas kernels for 0%

commit v1 on v0

--- a/solution.py
+++ b/solution.py
@@ -52,47 +52,25 @@
     w_up,
     w_down,
 ):
-    seq_rows = queries.shape[0]
     attended = attend(queries, keys, values, lengths)
-    projected = jnp.dot(
-        attended,
-        lax.all_gather(out_weight, "dev", axis=1, tiled=True),
-        preferred_element_type=jnp.float32,
-    ).astype(jnp.bfloat16)
+    attended_all = lax.all_gather(attended, "dev", axis=0, tiled=True)
+    columns = jnp.dot(attended_all, out_weight, preferred_element_type=jnp.float32).astype(
+        jnp.bfloat16
+    )
+    projected = lax.all_to_all(columns, "dev", split_axis=0, concat_axis=1, tiled=True)
     stream = residual.astype(jnp.float32) + projected.astype(jnp.float32)
     scale = lax.rsqrt(jnp.mean(stream * stream, axis=-1, keepdims=True) + 1e-06)
-    normalized_input = (stream * scale * norm_gain.astype(jnp.float32)).astype(jnp.bfloat16)
-    model_width = normalized_input.shape[1]
+    normed = (stream * scale * norm_gain.astype(jnp.float32)).astype(jnp.bfloat16)
     expert_count = lax.axis_size("dev")
-    selected_expert_count = expert_ids.shape[1]
-    capacity = 2 * seq_rows * selected_expert_count // expert_count
-    flattened_expert_index = expert_ids.reshape(-1)
-    one_hot = (
-        flattened_expert_index[:, None] == jnp.arange(expert_count, dtype=jnp.int32)[None, :]
-    ).astype(jnp.int32)
-    earlier = jnp.cumsum(one_hot, axis=0) - one_hot
-    slot_index = jnp.sum(earlier * one_hot, axis=1)
-    target = flattened_expert_index * capacity + slot_index
-    source_row = (
-        jnp.arange(seq_rows * selected_expert_count, dtype=jnp.int32) // selected_expert_count
-    )
-    packed = (
-        jnp.zeros((expert_count * capacity, model_width), jnp.bfloat16)
-        .at[target]
-        .set(normalized_input[source_row])
-    )
-    packed = packed.reshape(expert_count, capacity, model_width)
-    block = lax.all_to_all(packed, "dev", split_axis=0, concat_axis=0, tiled=True)
-    senders, slot_count, width = block.shape
-    result = expert_rows(block.reshape(senders * slot_count, width), w_gate, w_up, w_down)
-    result = result.reshape(senders, slot_count, width)
-    returned = lax.all_to_all(result, "dev", split_axis=0, concat_axis=0, tiled=True)
-    selected_experts = returned.reshape(expert_count * capacity, model_width)[target]
-    selected_experts = selected_experts.reshape(
-        seq_rows, selected_expert_count, model_width
-    ).astype(jnp.float32)
-    mixed_expert_output = jnp.einsum("cz,czw->cw", routed_gate_weight, selected_experts)
-    return (stream + mixed_expert_output).astype(jnp.bfloat16)
+    experts = jnp.arange(expert_count, dtype=jnp.int32)
+    named = expert_ids[:, :, None] == experts[None, None, :]
+    share = jnp.sum(jnp.where(named, routed_gate_weight[:, :, None], 0.0), axis=1)
+    mine = lax.all_to_all(share.T, "dev", split_axis=0, concat_axis=0, tiled=True).reshape(-1)
+    normed_all = lax.all_gather(normed, "dev", axis=0, tiled=True)
+    rows = expert_rows(normed_all, w_gate, w_up, w_down)
+    weighted = (rows.astype(jnp.float32) * mine[:, None]).astype(jnp.bfloat16)
+    mixed = lax.psum_scatter(weighted, "dev", scatter_dimension=0, tiled=True)
+    return (stream + mixed.astype(jnp.float32)).astype(jnp.bfloat16)
 
 
 def solution(mesh):

time: 450 us -> 243 us (0.54)
  the two profiles are of different devices: /device:TPU:13 before, /device:TPU:1 now
where the time goes in v1:
time: 243 us; the launch traced here: 240 us
  waiting for transfers between devices  171 us (70%)
  matrix products  36 us (15%)
  between operations  13.2 us (5%)
  blocking collectives  9.14 us (4%)
  other arithmetic  4.34 us (2%)
  starting transfers between devices  3.79 us (2%)
  local copies, waits for them, and re-layouts  2.48 us (1%)
    reduce_scatter x1, waiting for transfers between devices, per_device(): mixed = lax.psum_scatter(weighted, 'dev', scatter_dimension=0, tiled=True)  69.1 us
    all_gather x1, waiting for transfers between devices, per_device(): attended_all = lax.all_gather(attended, 'dev', axis=0, tiled=True)  53.2 us
    all_gather x1, waiting for transfers between devices, per_device(): normed_all = lax.all_gather(normed, 'dev', axis=0, tiled=True)  38.9 us
    dot_general x1, matrix products, expert_rows(): jnp.dot(inner, w_down[0], preferred_element_type=jnp.float32)  17 us
    all_to_all x1, waiting for transfers between devices, per_device(): lax.all_to_all(columns, 'dev', split_axis=0, concat_axis=1, tiled=True)  9.48 us
    all_to_all x1, blocking collectives, per_device(): lax.all_to_all(share.T, 'dev', split_axis=0, concat_axis=0, tiled=True)  9.14 us
    dot_general x1, matrix products, expert_rows(): jnp.dot(row_block, w_gate[0], preferred_element_type=jnp.float32)  8.7 us
  transfers between devices with their start and end apart: 4, of which 4 were waited for; matrix products, arithmetic and copies ran while one was open for 1% of the time, Pallas kernels for 0%

profile of v1, /device:TPU:1, one launch (start us, length us, event | category | flops | bytes accessed | tf_op | source)
XLA Modules:
  0.0 239.8 jit_solution(14443936847302265367)
XLA Ops:
  6.5 0.0 copy-start
  6.5 0.0 all-gather.3.cloned.1.call-start
  6.5 0.9 iota_compare_fusion.1
  7.4 1.0 copy.35
  8.4 0.0 copy-done
  8.4 2.6 %fusion.35 = (f32[32,2,16]{2,1,0:T(2,128)S(1)}, f32[32,2,16,160]{3,2,1,0:T(8,128)}) fusion(bf16[32,2,16,128]{3,2,1,0:T(8,128)(2,1)S(1)} %bitcast.68, pred[32,160]{1,0:T(8,128)(4,1)S(1)} %iota_compare_fusion.1, bf16[32,160,256]{2,1,0:T(8,128)(2,1)S(1)} %copy-done), kind=kOutput, calls=%fused_computation.35 | convolution fusion | flops 42598560 | bytes 3548160 | tf_op jit(solution)/shard_map/sub | solution.py:28
  11.0 2.9 %fusion.28 = bf16[32,2,16,128]{3,2,1,0:T(8,128)(2,1)S(1)} fusion(f32[32,2,16,160]{3,2,1,0:T(8,128)} %get-tuple-element.6, f32[32,2,16]{2,1,0:T(2,128)S(1)} %get-tuple-element.5, bf16[32,160,256]{2,1,0:T(8,128)(2,1)} %param.14), kind=kOutput, calls=%fused_computation.21 | convolution fusion | flops 42401792 | bytes 3543040 | tf_op jit(solution)/shard_map/bgqp,bpgd->bgqd/dot_general | solution.py:30
  13.9 0.8 copy.54
  14.7 0.0 all-gather.3.cloned.1.call-update
  14.8 0.0 copy-start.2
  14.8 0.0 copy-start.1
  14.8 53.2 %all-gather.3.cloned.1.call-done = bf16[512,4096]{1,0:T(8,128)(2,1)} async-done(((bf16[32,4096]{1,0:T(8,128)(2,1)}), bf16[512,4096]{1,0:T(8,128)(2,1)}) %all-gather.3.cloned.1.call-update) | async-done | bytes 4194320 | tf_op jit(solution)/shard_map/all_gather | solution.py:56
  68.0 4.8 %convolution_convert_fusion = bf16[512,256]{1,0:T(8,128)(2,1)} fusion(bf16[512,4096]{1,0:T(8,128)(2,1)} %all-gather.3.cloned.1.call-done, bf16[4096,256]{1,0:T(8,128)(2,1)} %param.17), kind=kOutput, calls=%fused_computation.20 | convolution fusion | flops 1073872896 | bytes 6553600 | tf_op jit(solution)/shard_map/dot_general | solution.py:57
  72.8 0.0 copy-start.3
  72.8 0.0 copy-start.4
  72.8 3.7 %all-to-all-start = ((bf16[16,32,256]{2,1,0:T(8,128)(2,1)}), bf16[16,32,256]{2,1,0:T(8,128)(2,1)S(1)}, u32[]{:S(2)}, u32[]{:S(2)}) async-start(bf16[16,32,256]{2,1,0:T(8,128)(2,1)} %bitcast), calls=%async_computation | async-start | bytes 524288 | tf_op jit(solution)/shard_map/all_to_all | solution.py:60
  76.5 0.0 all-gather.5.cloned.1.call-start
  76.6 0.0 copy-done.2
  76.6 9.5 %all-to-all-done = bf16[16,32,256]{2,1,0:T(8,128)(2,1)S(1)} async-done(((bf16[16,32,256]{2,1,0:T(8,128)(2,1)}), bf16[16,32,256]{2,1,0:T(8,128)(2,1)S(1)}, u32[]{:S(2)}, u32[]{:S(2)}) %all-to-all-start) | async-done | bytes 262176 | tf_op jit(solution)/shard_map/all_to_all | solution.py:60
  86.2 0.0 copy-done.1
  86.2 0.2 multiply_reduce_fusion
  86.4 0.8 multiply_convert_fusion.2
  87.2 0.0 all-gather.5.cloned.1.call-update
  87.2 0.0 reduce-scatter.2.cloned.1.call-start
  87.3 0.0 copy-done.3
  87.3 0.0 copy-done.4
  87.3 9.1 %all_to_all.22 = f32[16,1,32]{2,1,0:T(1,128)S(1)} all-to-all(f32[16,1,32]{2,1,0:T(1,128)S(1)} %bitcast.70), channel_id=1, replica_groups=mesh['groups'=2,'dev'=16] {'dev'}, dimensions={0} | all-to-all | bytes 4096 | tf_op jit(solution)/shard_map/all_to_all | solution.py:68
  96.5 0.5 broadcast.34
  97.0 0.6 reduce.3
  97.6 0.1 mul.51
  97.7 38.9 %all-gather.5.cloned.1.call-done = bf16[512,4096]{1,0:T(8,128)(2,1)} async-done(((bf16[32,4096]{1,0:T(8,128)(2,1)}), bf16[512,4096]{1,0:T(8,128)(2,1)}) %all-gather.5.cloned.1.call-update) | async-done | bytes 4194320 | tf_op jit(solution)/shard_map/all_gather | solution.py:69
  136.6 8.7 %fusion.5 = f32[512,768]{1,0:T(8,128)} fusion(bf16[512,4096]{1,0:T(8,128)(2,1)} %all-gather.5.cloned.1.call-done, bf16[1,4096,768]{2,1,0:T(8,128)(2,1)} %param.21), kind=kOutput, calls=%fused_computation.6 | convolution fusion | flops 3221225472 | bytes 12058624 | tf_op jit(solution)/shard_map/dot_general | solution.py:35
  145.3 17.0 %multiply_convert_fusion = bf16[512,4096]{1,0:T(8,128)(2,1)} fusion(bf16[1,768,4096]{2,1,0:T(8,128)(2,1)} %param.23, f32[512]{0:T(512)S(1)} %mul.51, f32[512,768]{1,0:T(8,128)} %fusion.5, bf16[512,4096]{1,0:T(8,128)(2,1)} %all-gather.5.cloned.1.call-done, bf16[1,4096,768]{2,1,0:T(8,128)(2,1)} %param.22), kind=kOutput, calls=%fused_computation.1 | convolution fusion | flops 6453198848 | bytes 22546432 | tf_op jit(solution)/shard_map/dot_general | solution.py:38
  162.4 0.0 reduce-scatter.2.cloned.1.call-update
  162.4 69.1 %reduce-scatter.2.cloned.1.call-done = bf16[32,4096]{1,0:T(8,128)(2,1)} async-done(((bf16[512,4096]{1,0:T(8,128)(2,1)}), bf16[32,4096]{1,0:T(8,128)(2,1)}) %reduce-scatter.2.cloned.1.call-update) | async-done | bytes 262160 | tf_op jit(solution)/shard_map/reduce_scatter | solution.py:72
  231.5 1.7 add_convert_fusion
  (5 shorter events, 0.1 us)
Async XLA Ops:
  6.5 1.9 copy-start
  6.5 61.4 %all-gather.3.cloned.1.call-start = ((), (), s32[]{:S(2)}) async-start(), calls=%async_computation.3 | async-start | bytes 4456448 | tf_op jit(solution)/shard_map/all_gather | solution.py:56
  14.8 61.8 %copy-start.2 = (bf16[4096]{0:T(1024)(128)(2,1)S(1)}, bf16[4096]{0:T(1024)(128)(2,1)}, u32[]{:S(2)}) copy-start(bf16[4096]{0:T(1024)(128)(2,1)} %param.18) | copy-start | bytes 24580
  14.8 71.4 %copy-start.1 = (bf16[32,4096]{1,0:T(8,128)(2,1)S(1)}, bf16[32,4096]{1,0:T(8,128)(2,1)}, u32[]{:S(2)}) copy-start(bf16[32,4096]{1,0:T(8,128)(2,1)} %param.16) | copy-start | bytes 786436
  72.8 14.5 %copy-start.3 = (f32[32,8]{0,1:T(8,128)S(1)}, f32[32,8]{0,1:T(8,128)}, u32[]{:S(2)}) copy-start(f32[32,8]{0,1:T(8,128)} %param.20) | copy-start | bytes 3076
  72.8 14.5 %copy-start.4 = (s32[32,8]{0,1:T(8,128)S(1)}, s32[32,8]{0,1:T(8,128)}, u32[]{:S(2)}) copy-start(s32[32,8]{0,1:T(8,128)} %param.19) | copy-start | bytes 3076
  72.8 13.3 %all-to-all-start = ((bf16[16,32,256]{2,1,0:T(8,128)(2,1)}), bf16[16,32,256]{2,1,0:T(8,128)(2,1)S(1)}, u32[]{:S(2)}, u32[]{:S(2)}) async-start(bf16[16,32,256]{2,1,0:T(8,128)(2,1)} %bitcast), calls=%async_computation | async-start | bytes 524288 | tf_op jit(solution)/shard_map/all_to_all | solution.py:60
  76.5 60.1 %all-gather.5.cloned.1.call-start = ((), (), s32[]{:S(2)}) async-start(), calls=%async_computation.4 | async-start | bytes 4456448 | tf_op jit(solution)/shard_map/all_gather | solution.py:69
  87.2 144.3 %reduce-scatter.2.cloned.1.call-start = ((), (), s32[]{:S(2)}) async-start(), calls=%async_computation.5 | async-start | bytes 4456448 | tf_op jit(solution)/shard_map/reduce_scatter | solution.py:72
Sparse Core Ops, SparseCore 0:
  14.9 53.0 all-gather.2
  87.3 49.2 all-gather.4
  162.5 68.9 reduce-scatter.1

commit v2 on v1

v2 whole, which is shorter than its diff:
```python
import functools
import math

import jax
import jax.numpy as jnp
from jax import lax
from jax.experimental import pallas as pl
from jax.experimental.pallas import tpu as pltpu
from jax.sharding import PartitionSpec as P

HQ = 32
KVH = 2
HD = 128


def attend(queries, keys, values, lengths):
    seq_rows = queries.shape[0]
    token_position_index = keys.shape[1]
    query_heads = queries.reshape(seq_rows, KVH, HQ // KVH, HD)
    key_heads = keys.reshape(seq_rows, token_position_index, KVH, HD)
    value_heads = values.reshape(seq_rows, token_position_index, KVH, HD)
    scores = jnp.einsum(
        "bgqd,bpgd->bgqp", query_heads, key_heads, preferred_element_type=jnp.float32
    ) * (1.0 / math.sqrt(HD))
    live = (
        jnp.arange(token_position_index, dtype=jnp.int32)[None, None, None, :]
        < lengths[:, None, None, None]
    )
    scores = jnp.where(live, scores, jnp.float32(-1e30))
    highest = jnp.max(scores, axis=-1, keepdims=True)
    weights = jnp.exp(scores - highest)
    probs = (weights / jnp.sum(weights, axis=-1, keepdims=True)).astype(jnp.bfloat16)
    mixed = jnp.einsum("bgqp,bpgd->bgqd", probs, value_heads, preferred_element_type=jnp.float32)
    return mixed.reshape(seq_rows, HQ * HD).astype(jnp.bfloat16)


MESH = pl.DeviceIdType.MESH
HALVES = 2
UP, DOWN, ACROSS, SIBLING = 0, 1, 2, 3


def layer_kernel(
    n,
    attended,
    residual,
    gain,
    share,
    out_weight,
    w_gate,
    w_up,
    w_down,
    out,
    rows_one,
    rows_two,
    cols,
    arrived,
    share_in,
    stream,
    inner,
    part,
    from_sib,
    from_y,
    from_below,
    from_above,
    v_out,
    v_gate,
    v_up,
    v_down,
    load_sem,
    send_one,
    recv_one,
    send_two,
    recv_two,
    col_send,
    col_recv,
    share_send,
    share_recv,
    sib_send,
    sib_recv,
    y_send,
    y_recv,
    up_send,
    up_recv,
    down_send,
    down_recv,
):
    me = lax.axis_index("dev")
    depth = n // 4
    z, y, k = me // 4, (me // 2) % 2, me % 2
    t_dev = attended.shape[0]
    half = t_dev // HALVES
    width = out_weight.shape[1]
    ff = w_gate.shape[1]
    model = attended.shape[1]

    def at(zz, yy, kk):
        return zz * 4 + yy * 2 + kk

    sib, beside = at(z, y, 1 - k), at(z, 1 - y, k)

    def remote(src, dst, send, recv, target):
        return pltpu.make_async_remote_copy(
            src_ref=src,
            dst_ref=dst,
            send_sem=send,
            recv_sem=recv,
            device_id={"dev": target},
            device_id_type=MESH,
        )

    loads = [
        pltpu.make_async_copy(out_weight, v_out, load_sem.at[0]),
        pltpu.make_async_copy(w_gate, v_gate, load_sem.at[1]),
        pltpu.make_async_copy(w_up, v_up, load_sem.at[2]),
        pltpu.make_async_copy(w_down, v_down, load_sem.at[3]),
    ]
    for load in loads:
        load.start()
    rows_one[me] = attended[...]

    barrier = pltpu.get_barrier_semaphore()

    def greet(i, _):
        pl.semaphore_signal(
            barrier, inc=1, device_id={"dev": lax.rem(me + i, n)}, device_id_type=MESH
        )
        return 0

    lax.fori_loop(1, n, greet, 0)
    pl.semaphore_wait(barrier, n - 1)

    def order(j):
        near = jnp.minimum(z, depth - 1 - z)
        both = j <= 2 * near
        dist = jnp.where(both, (j + 1) // 2, j - near)
        rising = jnp.where(z < depth - 1 - z, 1, -1)
        sign = jnp.where(both, jnp.where(j % 2 == 1, -1, 1), rising)
        return z + sign * dist

    def gather(buf, send, recv, use):
        def copy(b, h, way, target):
            piece = buf.at[b, pl.ds(h * half, half), :]
            return remote(piece, piece, send.at[b, h, way], recv.at[b, h], target)

        def sends(zj, b, h, act):
            @pl.when((zj <= z) & (z < depth - 1))
            def _():
                act(copy(b, h, UP, at(z + 1, y, k)))

            @pl.when((zj >= z) & (z > 0))
            def _():
                act(copy(b, h, DOWN, at(z - 1, y, k)))

            act(copy(b, h, ACROSS, beside))
            act(copy(b, h, SIBLING, sib))

        def stage(j, _):
            @pl.when(j < depth)
            def _():
                zj = order(j)
                b = at(zj, y, k)
                for h in range(HALVES):

                    @pl.when(j > 0)
                    def _():
                        copy(b, h, SIBLING, sib).wait_recv()

                    sends(zj, b, h, lambda c: c.start())

            @pl.when((j >= 1) & (j <= depth))
            def _():
                b = at(order(j - 1), 1 - y, k)
                for h in range(HALVES):
                    copy(b, h, SIBLING, sib).wait_recv()
                    copy(b, h, SIBLING, sib).start()

            @pl.when(j >= 2)
            def _():
                zj = order(j - 2)
                for yy in range(2):
                    for h in range(HALVES):
                        copy(at(zj, yy, 1 - k), h, SIBLING, sib).wait_recv()
                use(zj)

            return 0

        lax.fori_loop(0, depth + 2, stage, 0)

        def drain():
            def one(j, _):
                zj = order(j)
                for h in range(HALVES):
                    sends(zj, at(zj, y, k), h, lambda c: c.wait_send())
                    copy(at(zj, 1 - y, k), h, SIBLING, sib).wait_send()
                return 0

            lax.fori_loop(0, depth, one, 0)

        return drain

    def share_copy(b, slot):
        return remote(share.at[b], share_in.at[slot], share_send.at[b], share_recv.at[slot], b)

    def col_copy(b, slot):
        return remote(cols.at[b], arrived.at[slot], col_send.at[b], col_recv.at[slot], b)

    share_in[me] = share[me]

    def give_share(i, _):
        share_copy(lax.rem(me + i, n), me).start()
        return 0

    lax.fori_loop(1, n, give_share, 0)
    loads[0].wait()

    def project(zj):
        x = rows_one[pl.ds(zj * 4, 4)].reshape(4 * t_dev, model)
        c = jnp.dot(x, v_out[...], preferred_element_type=jnp.float32).astype(jnp.bfloat16)
        cols[pl.ds(zj * 4, 4)] = c.reshape(4, t_dev, width)
        for q in range(4):
            b = zj * 4 + q

            @pl.when(b != me)
            def _():
                col_copy(b, me).start()

    drain_one = gather(rows_one, send_one, recv_one, project)
    arrived[me] = cols[me]

    def take(i, _):
        s = lax.rem(me + i, n)
        col_copy(s, s).wait_recv()
        share_copy(s, s).wait_recv()
        return 0

    lax.fori_loop(1, n, take, 0)
    squares = jnp.zeros((t_dev, width), jnp.float32)
    for s in range(n):
        cut = pl.ds(s * width, width)
        piece = residual[:, cut].astype(jnp.float32) + arrived[s].astype(jnp.float32)
        stream[:, cut] = piece
        squares += piece * piece
    scale = lax.rsqrt(jnp.sum(squares, axis=1, keepdims=True) * (1.0 / model) + 1e-06)
    for s in range(n):
        cut = pl.ds(s * width, width)
        rows_two[me, :, cut] = (
            stream[:, cut] * scale * gain[:, cut].astype(jnp.float32)
        ).astype(jnp.bfloat16)
    for load in loads[1:]:
        load.wait()

    def sib_copy(b):
        return remote(part.at[b], from_sib.at[b], sib_send.at[b], sib_recv.at[b], sib)

    tile, wide = 256, 512
    lanes = share_in.shape[2]
    eye = lax.broadcasted_iota(jnp.int32, (t_dev, lanes), 0) == lax.broadcasted_iota(
        jnp.int32, (t_dev, lanes), 1
    )

    def expert(zj):
        def hidden(t, _):
            x = rows_two[pl.ds(zj * 4, 4)].reshape(4 * t_dev, model)
            cut = pl.ds(pl.multiple_of(t * tile, tile), tile)
            g = jnp.dot(x, v_gate[:, cut], preferred_element_type=jnp.float32)
            u = jnp.dot(x, v_up[:, cut], preferred_element_type=jnp.float32)
            inner[:, cut] = (g / (1.0 + jnp.exp(-g)) * u).astype(jnp.bfloat16)
            return 0

        lax.fori_loop(0, ff // tile, hidden, 0)
        weights = jnp.concatenate(
            [
                jnp.sum(
                    jnp.where(eye, share_in[zj * 4 + q, 0:1, :], 0.0), axis=1, keepdims=True
                )
                for q in range(4)
            ],
            axis=0,
        )

        def outward(t, _):
            cut = pl.ds(pl.multiple_of(t * wide, wide), wide)
            o = jnp.dot(inner[...], v_down[:, cut], preferred_element_type=jnp.float32)
            part[pl.ds(zj * 4, 4), :, cut] = (
                (o * weights).astype(jnp.bfloat16).reshape(4, t_dev, wide)
            )
            return 0

        lax.fori_loop(0, model // wide, outward, 0)
        for yy in range(2):
            sib_copy(at(zj, yy, 1 - k)).start()

    drain_two = gather(rows_two, send_two, recv_two, expert)

    def add(b, other):
        part[b] = (part[b].astype(jnp.float32) + other.astype(jnp.float32)).astype(jnp.bfloat16)

    def y_copy(zb):
        return remote(part.at[at(zb, 1 - y, k)], from_y.at[zb], y_send.at[zb], y_recv.at[zb], beside)

    def up_copy(zb):
        return remote(
            part.at[at(zb, y, k)], from_below.at[zb], up_send.at[zb], up_recv.at[zb], at(z + 1, y, k)
        )

    def down_copy(zb):
        return remote(
            part.at[at(zb, y, k)], from_above.at[zb], down_send.at[zb], down_recv.at[zb], at(z - 1, y, k)
        )

    def sides(t, act):
        @pl.when(z + t < depth)
        def _():
            act(z + t, True)

        @pl.when(z - t >= 0)
        def _():
            act(z - t, False)

    def cross(zb):
        for yy in (0, 1):
            sib_copy(at(zb, yy, k)).wait_recv()
        away = at(zb, 1 - y, k)
        add(away, from_sib[away])
        y_copy(zb).start()
        here = at(zb, y, k)
        add(here, from_sib[here])

    def cross_level(i, _):
        sides(depth - 1 - i, lambda zb, rising: cross(zb))
        return 0

    lax.fori_loop(0, depth - 1, cross_level, 0)
    cross(z)

    def along(zb, rising):
        y_copy(zb).wait_recv()
        here = at(zb, y, k)
        add(here, from_y[zb])
        if rising:

            @pl.when(z > 0)
            def _():
                up_copy(zb).wait_recv()
                add(here, from_below[zb])

            up_copy(zb).start()
        else:

            @pl.when(z < depth - 1)
            def _():
                down_copy(zb).wait_recv()
                add(here, from_above[zb])

            down_copy(zb).start()

    def along_level(i, _):
        sides(depth - 1 - i, along)
        return 0

    lax.fori_loop(0, depth - 1, along_level, 0)
    y_copy(z).wait_recv()
    stream[...] += part[me].astype(jnp.float32) + from_y[z].astype(jnp.float32)

    @pl.when(z > 0)
    def _():
        up_copy(z).wait_recv()
        stream[...] += from_below[z].astype(jnp.float32)

    @pl.when(z < depth - 1)
    def _():
        down_copy(z).wait_recv()
        stream[...] += from_above[z].astype(jnp.float32)

    out[...] = stream[...].astype(jnp.bfloat16)

    drain_one()
    drain_two()

    def sent(i, _):
        b = lax.rem(me + i, n)
        share_copy(b, me).wait_send()
        col_copy(b, me).wait_send()
        return 0

    lax.fori_loop(1, n, sent, 0)

    def sent_line(zb, _):
        for yy in range(2):
            sib_copy(at(zb, yy, 1 - k)).wait_send()
        y_copy(zb).wait_send()

        @pl.when(zb > z)
        def _():
            up_copy(zb).wait_send()

        @pl.when(zb < z)
        def _():
            down_copy(zb).wait_send()

        return 0

    lax.fori_loop(0, depth, sent_line, 0)


def per_device(
    queries,
    keys,
    values,
    lengths,
    residual,
    out_weight,
    norm_gain,
    expert_ids,
    routed_gate_weight,
    w_gate,
    w_up,
    w_down,
):
    n = lax.axis_size("dev")
    depth = n // 4
    t_dev, model = residual.shape
    width = out_weight.shape[1]
    ff = w_gate.shape[2]
    attended = attend(queries, keys, values, lengths)
    experts = jnp.arange(n, dtype=jnp.int32)
    named = expert_ids[None, :, :] == experts[:, None, None]
    share = jnp.sum(jnp.where(named, routed_gate_weight[None], 0.0), axis=2)
    share = jnp.zeros((n, 8, 128), jnp.float32).at[:, 0, :t_dev].set(share)
    vmem, anywhere = pl.BlockSpec(memory_space=pltpu.VMEM), pl.BlockSpec(memory_space=pl.ANY)
    b16, f32 = jnp.bfloat16, jnp.float32
    dma = pltpu.SemaphoreType.DMA
    return pl.pallas_call(
        functools.partial(layer_kernel, n),
        out_shape=jax.ShapeDtypeStruct((t_dev, model), b16),
        in_specs=[vmem] * 4 + [anywhere] * 4,
        out_specs=vmem,
        scratch_shapes=[
            pltpu.VMEM((n, t_dev, model), b16),
            pltpu.VMEM((n, t_dev, model), b16),
            pltpu.VMEM((n, t_dev, width), b16),
            pltpu.VMEM((n, t_dev, width), b16),
            pltpu.VMEM((n, 8, 128), f32),
            pltpu.VMEM((t_dev, model), f32),
            pltpu.VMEM((4 * t_dev, ff), b16),
            pltpu.VMEM((n, t_dev, model), b16),
            pltpu.VMEM((n, t_dev, model), b16),
            pltpu.VMEM((depth, t_dev, model), b16),
            pltpu.VMEM((depth, t_dev, model), b16),
            pltpu.VMEM((depth, t_dev, model), b16),
            pltpu.VMEM((model, width), b16),
            pltpu.VMEM((model, ff), b16),
            pltpu.VMEM((model, ff), b16),
            pltpu.VMEM((ff, model), b16),
            dma((4,)),
            dma((n, HALVES, 4)),
            dma((n, HALVES)),
            dma((n, HALVES, 4)),
            dma((n, HALVES)),
            dma((n,)),
            dma((n,)),
            dma((n,)),
            dma((n,)),
            dma((n,)),
            dma((n,)),
            dma((depth,)),
            dma((depth,)),
            dma((depth,)),
            dma((depth,)),
            dma((depth,)),
            dma((depth,)),
        ],
        compiler_params=pltpu.CompilerParams(
            collective_id=0, has_side_effects=True, vmem_limit_bytes=62 * 1024 * 1024
        ),
    )(
        attended,
        residual,
        norm_gain.reshape(1, model),
        share,
        out_weight,
        w_gate[0],
        w_up[0],
        w_down[0],
    )


def solution(mesh):
    in_specs = (
        P(("groups", "dev"), None),
        P(("groups", "dev"), None, None),
        P(("groups", "dev"), None, None),
        P(("groups", "dev")),
        P(("groups", "dev"), None),
        P(None, "dev"),
        P(),
        P(("groups", "dev"), None),
        P(("groups", "dev"), None),
        P("dev", None, None),
        P("dev", None, None),
        P("dev", None, None),
    )
    out_specs = P(("groups", "dev"), None)
    return jax.shard_map(
        per_device, mesh=mesh, in_specs=in_specs, out_specs=out_specs, check_vma=False
    )
```

time: 243 us -> 128 us (0.53)
  waiting for transfers between devices: 171 us -> 0 us
  Pallas kernels: 0 us -> 115 us
  matrix products: 36 us -> 6.39 us
  between operations: 13.2 us -> 0.06 us
  blocking collectives: 9.14 us -> 0 us
  starting transfers between devices: 3.79 us -> 0 us
  other arithmetic: 4.34 us -> 0.76 us
    pallas_call x0 -> x1, Pallas kernels: none -> 115 us  [per_device(): pl.pallas_call(functools.partial(layer_kernel, n), out_shape=jax.ShapeDty...]
    all_gather x2 -> x0, waiting for transfers between devices: 92.1 us -> none  [the longest x1 53.2 us: per_device(): attended_all = lax.all_gather(attended, 'dev', axis=0, tiled=True)]
    reduce_scatter x1 -> x0, waiting for transfers between devices: 69.1 us -> none  [per_device(): mixed = lax.psum_scatter(weighted, 'dev', scatter_dimension=0, tiled=True)]
    dot_general x3 -> x0, matrix products: 30.5 us -> none  [the longest x1 17 us: expert_rows(): jnp.dot(inner, w_down[0], preferred_element_type=jnp.float32)]
    all_to_all x1 -> x0, waiting for transfers between devices: 9.48 us -> none  [per_device(): lax.all_to_all(columns, 'dev', split_axis=0, concat_axis=1, tiled=True)]
    all_to_all x1 -> x0, blocking collectives: 9.14 us -> none  [per_device(): lax.all_to_all(share.T, 'dev', split_axis=0, concat_axis=0, tiled=True)]
    all_to_all x1 -> x0, starting transfers between devices: 3.71 us -> none  [per_device(): lax.all_to_all(columns, 'dev', split_axis=0, concat_axis=1, tiled=True)]
    convert_element_type x3 -> x0, other arithmetic: 2.57 us -> none  [the longest x1 1.73 us: per_device(): return (stream + mixed.astype(jnp.float32)).astype(jnp.bfloat16)]
  transfers between devices with their start and end apart: 4 -> 0, of which waited for: 4 -> 0; matrix products, arithmetic and copies ran while one was open for 1% -> 0% of each run, Pallas kernels for 0% -> 0%
where the time goes in v2:
time: 128 us; the launch traced here: 127 us
  Pallas kernels  115 us (90%)
  matrix products  6.39 us (5%)
  local copies, waits for them, and re-layouts  4.89 us (4%)
    pallas_call x1, Pallas kernels, per_device(): pl.pallas_call(functools.partial(layer_kernel, n), out_shape=jax.ShapeDty...  115 us
    sub x1, matrix products, attend(): weights = jnp.exp(scores - highest)  4.32 us
    unnamed x11, local copies, waits for them, and re-layouts  3.66 us

profile of v2, /device:TPU:1, one launch (start us, length us, event | category | flops | bytes accessed | tf_op | source)
XLA Modules:
  0.0 126.8 jit_solution(5400197662803387653)
XLA Ops:
  0.0 0.0 copy-start.3
  0.0 1.1 copy.21
  1.1 0.7 iota_compare_fusion.1
  1.9 4.3 %fusion.19 = (f32[32,2,16]{2,1,0:T(2,128)S(1)}, f32[32,2,16,160]{3,2,1,0:T(8,128)}) fusion(bf16[32,2,16,128]{3,2,1,0:T(8,128)(2,1)S(1)} %bitcast.41, pred[32,160]{1,0:T(8,128)(4,1)S(1)} %iota_compare_fusion.1, bf16[32,160,256]{2,1,0:T(8,128)(2,1)} %param.15), kind=kOutput, calls=%fused_computation.18 | convolution fusion | flops 42598560 | bytes 3548160 | tf_op jit(solution)/shard_map/sub | solution.py:31
  6.2 0.0 copy-done.3
  6.2 0.0 copy-start.1
  6.2 0.0 copy-start.2
  6.2 0.0 copy-start
  6.2 2.1 %fusion.15 = bf16[32,2,16,128]{3,2,1,0:T(8,128)(2,1)S(1)} fusion(f32[32,2,16,160]{3,2,1,0:T(8,128)} %get-tuple-element.18, f32[32,2,16]{2,1,0:T(2,128)S(1)} %get-tuple-element.17, bf16[32,160,256]{2,1,0:T(8,128)(2,1)S(1)} %copy-done.3), kind=kOutput, calls=%fused_computation.11 | convolution fusion | flops 42401792 | bytes 3543040 | tf_op jit(solution)/shard_map/bgqp,bpgd->bgqd/dot_general | solution.py:33
  8.3 0.8 copy.40
  9.2 0.0 copy-done.1
  9.2 0.0 copy-done.2
  9.2 0.6 scatter.4.share
  9.8 0.0 copy-done
  9.8 0.6 reshape.80.gain
  10.4 114.6 %shard_map.118 = bf16[32,4096]{1,0:T(8,128)(2,1)} custom-call(bf16[32,4096]{1,0:T(8,128)(2,1)} %bitcast.39, bf16[32,4096]{1,0:T(8,128)(2,1)} %residual.1, bf16[1,4096]{1,0:T(2,128)(2,1)} %reshape.80.gain, f32[16,8,128]{2,1,0:T(8,128)} %scatter.4.share, bf16[4096,256]{1,0:T(8,128)(2,1)} %out_weight.1, bf16[4096,768]{1,0:T(8,128)(2,1)} %bitcast.36, ...), custom_call_target="tpu_custom_call" | custom-call | tf_op jit(solution)/shard_map/pallas_call | solution.py:433
  125.1 1.7 %copy.42 = bf16[32,4096]{1,0:T(8,128)(2,1)} copy(bf16[32,4096]{1,0:T(8,128)(2,1)} %shard_map.118) | data formatting | bytes 524288
  (1 shorter events, 0.0 us)
Async XLA Ops:
  0.0 6.2 %copy-start.3 = (bf16[32,160,256]{2,1,0:T(8,128)(2,1)S(1)}, bf16[32,160,256]{2,1,0:T(8,128)(2,1)}, u32[]{:S(2)}) copy-start(bf16[32,160,256]{2,1,0:T(8,128)(2,1)} %param.16) | copy-start | bytes 7864324
  6.2 2.9 %copy-start.1 = (f32[32,8]{0,1:T(8,128)S(1)}, f32[32,8]{0,1:T(8,128)}, u32[]{:S(2)}) copy-start(f32[32,8]{0,1:T(8,128)} %param.22) | copy-start | bytes 3076
  6.2 2.9 %copy-start.2 = (s32[32,8]{0,1:T(8,128)S(1)}, s32[32,8]{0,1:T(8,128)}, u32[]{:S(2)}) copy-start(s32[32,8]{0,1:T(8,128)} %param.21) | copy-start | bytes 3076
  6.2 3.6 %copy-start = (bf16[4096]{0:T(1024)(128)(2,1)S(1)}, bf16[4096]{0:T(1024)(128)(2,1)}, u32[]{:S(2)}) copy-start(bf16[4096]{0:T(1024)(128)(2,1)} %param.20) | copy-start | bytes 24580

commit v3 on v2

--- a/solution.py
+++ b/solution.py
@@ -155,11 +155,12 @@
             act(copy(b, h, SIBLING, sib))
 
         def stage(j, _):
-            @pl.when(j < depth)
-            def _():
-                zj = order(j)
-                b = at(zj, y, k)
-                for h in range(HALVES):
+            for h in range(HALVES):
+
+                @pl.when(j < depth)
+                def _():
+                    zj = order(j)
+                    b = at(zj, y, k)
 
                     @pl.when(j > 0)
                     def _():
@@ -167,20 +168,20 @@
 
                     sends(zj, b, h, lambda c: c.start())
 
-            @pl.when((j >= 1) & (j <= depth))
-            def _():
-                b = at(order(j - 1), 1 - y, k)
-                for h in range(HALVES):
+                @pl.when((j >= 1) & (j <= depth))
+                def _():
+                    b = at(order(j - 1), 1 - y, k)
                     copy(b, h, SIBLING, sib).wait_recv()
                     copy(b, h, SIBLING, sib).start()
 
-            @pl.when(j >= 2)
-            def _():
-                zj = order(j - 2)
-                for yy in range(2):
-                    for h in range(HALVES):
-                        copy(at(zj, yy, 1 - k), h, SIBLING, sib).wait_recv()
-                use(zj)
+                @pl.when(j >= 2)
+                def _():
+                    zj = order(j - 2)
+                    if h == 0:
+                        for yy in range(2):
+                            for hh in range(HALVES):
+                                copy(at(zj, yy, 1 - k), hh, SIBLING, sib).wait_recv()
+                    use(zj, h)
 
             return 0
 
@@ -213,7 +214,9 @@
     lax.fori_loop(1, n, give_share, 0)
     loads[0].wait()
 
-    def project(zj):
+    def project(zj, h):
+        if h > 0:
+            return
         x = rows_one[pl.ds(zj * 4, 4)].reshape(4 * t_dev, model)
         c = jnp.dot(x, v_out[...], preferred_element_type=jnp.float32).astype(jnp.bfloat16)
         cols[pl.ds(zj * 4, 4)] = c.reshape(4, t_dev, width)
@@ -250,7 +253,7 @@
         load.wait()
 
     def sib_copy(b):
-        return remote(part.at[b], from_sib.at[b], sib_send.at[b], sib_recv.at[b], sib)
+        return remote(part.at[b], from_sib.at[b // 2], sib_send.at[b // 2], sib_recv.at[b // 2], sib)
 
     tile, wide = 256, 512
     lanes = share_in.shape[2]
@@ -258,7 +261,7 @@
         jnp.int32, (t_dev, lanes), 1
     )
 
-    def expert(zj):
+    def expert(zj, h):
         def hidden(t, _):
             x = rows_two[pl.ds(zj * 4, 4)].reshape(4 * t_dev, model)
             cut = pl.ds(pl.multiple_of(t * tile, tile), tile)
@@ -267,7 +270,9 @@
             inner[:, cut] = (g / (1.0 + jnp.exp(-g)) * u).astype(jnp.bfloat16)
             return 0
 
-        lax.fori_loop(0, ff // tile, hidden, 0)
+        if h == 0:
+            lax.fori_loop(0, ff // tile, hidden, 0)
+            return
         weights = jnp.concatenate(
             [
                 jnp.sum(
@@ -292,84 +297,122 @@
 
     drain_two = gather(rows_two, send_two, recv_two, expert)
 
-    def add(b, other):
-        part[b] = (part[b].astype(jnp.float32) + other.astype(jnp.float32)).astype(jnp.bfloat16)
-
-    def y_copy(zb):
-        return remote(part.at[at(zb, 1 - y, k)], from_y.at[zb], y_send.at[zb], y_recv.at[zb], beside)
-
-    def up_copy(zb):
+    def cut_rows(h):
+        return pl.ds(h * half, half)
+
+    def add(b, h, other):
+        rows = cut_rows(h)
+        part[b, rows, :] = (
+            part[b, rows, :].astype(jnp.float32) + other.astype(jnp.float32)
+        ).astype(jnp.bfloat16)
+
+    def line_copy(src, dst, send, recv, zb, h, target):
+        rows = cut_rows(h)
         return remote(
-            part.at[at(zb, y, k)], from_below.at[zb], up_send.at[zb], up_recv.at[zb], at(z + 1, y, k)
+            part.at[src, rows, :], dst.at[zb, rows, :], send.at[zb, h], recv.at[zb, h], target
         )
 
-    def down_copy(zb):
-        return remote(
-            part.at[at(zb, y, k)], from_above.at[zb], down_send.at[zb], down_recv.at[zb], at(z - 1, y, k)
-        )
+    def y_copy(zb, h):
+        return line_copy(at(zb, 1 - y, k), from_y, y_send, y_recv, zb, h, beside)
+
+    def up_copy(zb, h):
+        return line_copy(at(zb, y, k), from_below, up_send, up_recv, zb, h, at(z + 1, y, k))
+
+    def down_copy(zb, h):
+        return line_copy(at(zb, y, k), from_above, down_send, down_recv, zb, h, at(z - 1, y, k))
 
     def sides(t, act):
-        @pl.when(z + t < depth)
-        def _():
-            act(z + t, True)
-
-        @pl.when(z - t >= 0)
-        def _():
-            act(z - t, False)
-
-    def cross(zb):
-        for yy in (0, 1):
-            sib_copy(at(zb, yy, k)).wait_recv()
-        away = at(zb, 1 - y, k)
-        add(away, from_sib[away])
-        y_copy(zb).start()
+        for h in range(HALVES):
+
+            @pl.when(z + t < depth)
+            def _():
+                act(z + t, h, True)
+
+            @pl.when(z - t >= 0)
+            def _():
+                act(z - t, h, False)
+
+    def cross(zb, h):
+        away, here = at(zb, 1 - y, k), at(zb, y, k)
+        if h == 0:
+            sib_copy(away).wait_recv()
+        add(away, h, from_sib[zb * 2 + 1 - y, cut_rows(h), :])
+        y_copy(zb, h).start()
+
+    def cross_level(i, _):
+        sides(depth - 1 - i, lambda zb, h, rising: cross(zb, h))
+        return 0
+
+    lax.fori_loop(0, depth - 1, cross_level, 0)
+    for h in range(HALVES):
+        cross(z, h)
+
+    def home(zb, _):
         here = at(zb, y, k)
-        add(here, from_sib[here])
-
-    def cross_level(i, _):
-        sides(depth - 1 - i, lambda zb, rising: cross(zb))
-        return 0
-
-    lax.fori_loop(0, depth - 1, cross_level, 0)
-    cross(z)
-
-    def along(zb, rising):
-        y_copy(zb).wait_recv()
-        here = at(zb, y, k)
-        add(here, from_y[zb])
+        sib_copy(here).wait_recv()
+        for h in range(HALVES):
+            add(here, h, from_sib[zb * 2 + y, cut_rows(h), :])
+        return 0
+
+    lax.fori_loop(0, depth, home, 0)
+
+    def along(zb, h, rising):
+        y_copy(zb, h).wait_recv()
+        here, rows = at(zb, y, k), cut_rows(h)
         if rising:
 
+            @pl.when(z == 0)
+            def _():
+                add(here, h, from_y[zb, rows, :])
+
             @pl.when(z > 0)
             def _():
-                up_copy(zb).wait_recv()
-                add(here, from_below[zb])
-
-            up_copy(zb).start()
+                up_copy(zb, h).wait_recv()
+                add(
+                    here,
+                    h,
+                    from_y[zb, rows, :].astype(jnp.float32)
+                    + from_below[zb, rows, :].astype(jnp.float32),
+                )
+
+            up_copy(zb, h).start()
         else:
 
+            @pl.when(z == depth - 1)
+            def _():
+                add(here, h, from_y[zb, rows, :])
+
             @pl.when(z < depth - 1)
             def _():
-                down_copy(zb).wait_recv()
-                add(here, from_above[zb])
-
-            down_copy(zb).start()
+                down_copy(zb, h).wait_recv()
+                add(
+                    here,
+                    h,
+                    from_y[zb, rows, :].astype(jnp.float32)
+                    + from_above[zb, rows, :].astype(jnp.float32),
+                )
+
+            down_copy(zb, h).start()
 
     def along_level(i, _):
         sides(depth - 1 - i, along)
         return 0
 
     lax.fori_loop(0, depth - 1, along_level, 0)
-    y_copy(z).wait_recv()
+    for h in range(HALVES):
+        y_copy(z, h).wait_recv()
     stream[...] += part[me].astype(jnp.float32) + from_y[z].astype(jnp.float32)
 
     @pl.when(z > 0)
     def _():
-        up_copy(z).wait_recv()
+        for h in range(HALVES):
+            up_copy(z, h).wait_recv()
         stream[...] += from_below[z].astype(jnp.float32)
 
     @pl.when(z < depth - 1)
     def _():
-        down_copy(z).wait_recv()
+        for h in range(HALVES):
+            down_copy(z, h).wait_recv()
         stream[...] += from_above[z].astype(jnp.float32)
 
     out[...] = stream[...].astype(jnp.bfloat16)
@@ -388,15 +431,16 @@
     def sent_line(zb, _):
         for yy in range(2):
             sib_copy(at(zb, yy, 1 - k)).wait_send()
-        y_copy(zb).wait_send()
-
-        @pl.when(zb > z)
-        def _():
-            up_copy(zb).wait_send()
-
-        @pl.when(zb < z)
-        def _():
-            down_copy(zb).wait_send()
+        for h in range(HALVES):
+            y_copy(zb, h).wait_send()
+
+            @pl.when(zb > z)
+            def _():
+                up_copy(zb, h).wait_send()
+
+            @pl.when(zb < z)
+            def _():
+                down_copy(zb, h).wait_send()
 
         return 0
 
@@ -444,7 +488,7 @@
             pltpu.VMEM((t_dev, model), f32),
             pltpu.VMEM((4 * t_dev, ff), b16),
             pltpu.VMEM((n, t_dev, model), b16),
-            pltpu.VMEM((n, t_dev, model), b16),
+            pltpu.VMEM((n // 2, t_dev, model), b16),
             pltpu.VMEM((depth, t_dev, model), b16),
             pltpu.VMEM((depth, t_dev, model), b16),
             pltpu.VMEM((depth, t_dev, model), b16),
@@ -461,14 +505,14 @@
             dma((n,)),
             dma((n,)),
             dma((n,)),
-            dma((n,)),
-            dma((n,)),
-            dma((depth,)),
-            dma((depth,)),
-            dma((depth,)),
-            dma((depth,)),
-            dma((depth,)),
-            dma((depth,)),
+            dma((n // 2,)),
+            dma((n // 2,)),
+            dma((depth, HALVES)),
+            dma((depth, HALVES)),
+            dma((depth, HALVES)),
+            dma((depth, HALVES)),
+            dma((depth, HALVES)),
+            dma((depth, HALVES)),
         ],
         compiler_params=pltpu.CompilerParams(
             collective_id=0, has_side_effects=True, vmem_limit_bytes=62 * 1024 * 1024

time: 128 us -> 117 us (0.914)
  Pallas kernels: 115 us -> 104 us
    pallas_call x1, Pallas kernels: 115 us -> 104 us  [per_device(): pl.pallas_call(functools.partial(layer_kernel, n), out_shape=jax.ShapeDty...]
where the time goes in v3:
time: 117 us; the launch traced here: 116 us
  Pallas kernels  104 us (89%)
  matrix products  6.39 us (5%)
  local copies, waits for them, and re-layouts  4.89 us (4%)
    pallas_call x1, Pallas kernels, per_device(): pl.pallas_call(functools.partial(layer_kernel, n), out_shape=jax.ShapeDty...  104 us
    sub x1, matrix products, attend(): weights = jnp.exp(scores - highest)  4.32 us
    unnamed x11, local copies, waits for them, and re-layouts  3.66 us

profile of v3, /device:TPU:1, one launch (start us, length us, event | category | flops | bytes accessed | tf_op | source)
XLA Modules:
  0.0 116.4 jit_solution(13501995059930215278)
XLA Ops:
  0.0 0.0 copy-start.3
  0.0 1.1 copy.21
  1.1 0.7 iota_compare_fusion.1
  1.9 4.3 %fusion.19 = (f32[32,2,16]{2,1,0:T(2,128)S(1)}, f32[32,2,16,160]{3,2,1,0:T(8,128)}) fusion(bf16[32,2,16,128]{3,2,1,0:T(8,128)(2,1)S(1)} %bitcast.41, pred[32,160]{1,0:T(8,128)(4,1)S(1)} %iota_compare_fusion.1, bf16[32,160,256]{2,1,0:T(8,128)(2,1)} %param.15), kind=kOutput, calls=%fused_computation.18 | convolution fusion | flops 42598560 | bytes 3548160 | tf_op jit(solution)/shard_map/sub | solution.py:31
  6.2 0.0 copy-done.3
  6.2 0.0 copy-start.1
  6.2 0.0 copy-start.2
  6.2 0.0 copy-start
  6.2 2.1 %fusion.15 = bf16[32,2,16,128]{3,2,1,0:T(8,128)(2,1)S(1)} fusion(f32[32,2,16,160]{3,2,1,0:T(8,128)} %get-tuple-element.18, f32[32,2,16]{2,1,0:T(2,128)S(1)} %get-tuple-element.17, bf16[32,160,256]{2,1,0:T(8,128)(2,1)S(1)} %copy-done.3), kind=kOutput, calls=%fused_computation.11 | convolution fusion | flops 42401792 | bytes 3543040 | tf_op jit(solution)/shard_map/bgqp,bpgd->bgqd/dot_general | solution.py:33
  8.3 0.8 copy.40
  9.2 0.0 copy-done.1
  9.2 0.0 copy-done.2
  9.2 0.6 scatter.4.share
  9.8 0.0 copy-done
  9.8 0.6 reshape.80.gain
  10.4 104.3 %shard_map.118 = bf16[32,4096]{1,0:T(8,128)(2,1)} custom-call(bf16[32,4096]{1,0:T(8,128)(2,1)} %bitcast.39, bf16[32,4096]{1,0:T(8,128)(2,1)} %residual.1, bf16[1,4096]{1,0:T(2,128)(2,1)} %reshape.80.gain, f32[16,8,128]{2,1,0:T(8,128)} %scatter.4.share, bf16[4096,256]{1,0:T(8,128)(2,1)} %out_weight.1, bf16[4096,768]{1,0:T(8,128)(2,1)} %bitcast.36, ...), custom_call_target="tpu_custom_call" | custom-call | tf_op jit(solution)/shard_map/pallas_call | solution.py:477
  114.7 1.7 %copy.42 = bf16[32,4096]{1,0:T(8,128)(2,1)} copy(bf16[32,4096]{1,0:T(8,128)(2,1)} %shard_map.118) | data formatting | bytes 524288
  (1 shorter events, 0.0 us)
Async XLA Ops:
  0.0 6.2 %copy-start.3 = (bf16[32,160,256]{2,1,0:T(8,128)(2,1)S(1)}, bf16[32,160,256]{2,1,0:T(8,128)(2,1)}, u32[]{:S(2)}) copy-start(bf16[32,160,256]{2,1,0:T(8,128)(2,1)} %param.16) | copy-start | bytes 7864324
  6.2 2.9 %copy-start.1 = (f32[32,8]{0,1:T(8,128)S(1)}, f32[32,8]{0,1:T(8,128)}, u32[]{:S(2)}) copy-start(f32[32,8]{0,1:T(8,128)} %param.22) | copy-start | bytes 3076
  6.2 2.9 %copy-start.2 = (s32[32,8]{0,1:T(8,128)S(1)}, s32[32,8]{0,1:T(8,128)}, u32[]{:S(2)}) copy-start(s32[32,8]{0,1:T(8,128)} %param.21) | copy-start | bytes 3076
  6.2 3.6 %copy-start = (bf16[4096]{0:T(1024)(128)(2,1)S(1)}, bf16[4096]{0:T(1024)(128)(2,1)}, u32[]{:S(2)}) copy-start(bf16[4096]{0:T(1024)(128)(2,1)} %param.20) | copy-start | bytes 24580

commit v4 on v3

--- a/solution.py
+++ b/solution.py
@@ -13,43 +13,32 @@
 HD = 128
 
 
-def attend(queries, keys, values, lengths):
-    seq_rows = queries.shape[0]
-    token_position_index = keys.shape[1]
-    query_heads = queries.reshape(seq_rows, KVH, HQ // KVH, HD)
-    key_heads = keys.reshape(seq_rows, token_position_index, KVH, HD)
-    value_heads = values.reshape(seq_rows, token_position_index, KVH, HD)
-    scores = jnp.einsum(
-        "bgqd,bpgd->bgqp", query_heads, key_heads, preferred_element_type=jnp.float32
-    ) * (1.0 / math.sqrt(HD))
-    live = (
-        jnp.arange(token_position_index, dtype=jnp.int32)[None, None, None, :]
-        < lengths[:, None, None, None]
-    )
-    scores = jnp.where(live, scores, jnp.float32(-1e30))
-    highest = jnp.max(scores, axis=-1, keepdims=True)
-    weights = jnp.exp(scores - highest)
-    probs = (weights / jnp.sum(weights, axis=-1, keepdims=True)).astype(jnp.bfloat16)
-    mixed = jnp.einsum("bgqp,bpgd->bgqd", probs, value_heads, preferred_element_type=jnp.float32)
-    return mixed.reshape(seq_rows, HQ * HD).astype(jnp.bfloat16)
-
-
 MESH = pl.DeviceIdType.MESH
 HALVES = 2
+TOGETHER = 8
 UP, DOWN, ACROSS, SIBLING = 0, 1, 2, 3
 
 
 def layer_kernel(
     n,
-    attended,
+    lengths,
+    queries,
     residual,
     gain,
-    share,
+    ids,
+    routed,
+    keys,
+    values,
     out_weight,
     w_gate,
     w_up,
     w_down,
     out,
+    heads_in,
+    heads_out,
+    v_keys,
+    v_values,
+    share,
     rows_one,
     rows_two,
     cols,
@@ -67,6 +56,7 @@
     v_up,
     v_down,
     load_sem,
+    kv_sem,
     send_one,
     recv_one,
     send_two,
@@ -87,11 +77,13 @@
     me = lax.axis_index("dev")
     depth = n // 4
     z, y, k = me // 4, (me // 2) % 2, me % 2
-    t_dev = attended.shape[0]
+    t_dev = queries.shape[0]
     half = t_dev // HALVES
     width = out_weight.shape[1]
     ff = w_gate.shape[1]
-    model = attended.shape[1]
+    model = queries.shape[1]
+    positions = keys.shape[1]
+    groups = HQ // KVH
 
     def at(zz, yy, kk):
         return zz * 4 + yy * 2 + kk
@@ -114,9 +106,18 @@
         pltpu.make_async_copy(w_up, v_up, load_sem.at[2]),
         pltpu.make_async_copy(w_down, v_down, load_sem.at[3]),
     ]
+    def kv_loads(h):
+        rows = pl.ds(h * half, half)
+        return (
+            pltpu.make_async_copy(keys.at[rows], v_keys.at[rows], kv_sem.at[h, 0]),
+            pltpu.make_async_copy(values.at[rows], v_values.at[rows], kv_sem.at[h, 1]),
+        )
+
+    for h in range(HALVES):
+        for load in kv_loads(h):
+            load.start()
     for load in loads:
         load.start()
-    rows_one[me] = attended[...]
 
     barrier = pltpu.get_barrier_semaphore()
 
@@ -127,6 +128,47 @@
         return 0
 
     lax.fori_loop(1, n, greet, 0)
+
+    expert_lane = lax.broadcasted_iota(jnp.int32, (t_dev, 128), 1)
+    dense = jnp.zeros((t_dev, 128), jnp.float32)
+    for i in range(ids.shape[1]):
+        dense += jnp.where(ids[:, i : i + 1] == expert_lane, routed[:, i : i + 1], 0.0)
+    turned = jnp.concatenate([dense, jnp.zeros((128 - t_dev, 128), jnp.float32)], axis=0).T
+    for e in range(n):
+        share[e] = jnp.broadcast_to(turned[e : e + 1, :], (8, 128))
+
+    for i in range(HQ):
+        heads_in[:, i, :] = queries[:, i * HD : (i + 1) * HD].astype(jnp.float32)
+
+    def attend_half(h):
+        for load in kv_loads(h):
+            load.wait()
+        low = lax.broadcasted_iota(jnp.int32, (HQ, HD), 0) < groups
+        place = lax.broadcasted_iota(jnp.int32, (HQ, positions), 1)
+
+        def some(i, _):
+            for u in range(TOGETHER):
+                b = h * half + i * TOGETHER + u
+                q = heads_in[b]
+                q = jnp.concatenate(
+                    [jnp.where(low, q, 0.0), jnp.where(low, 0.0, q)], axis=1
+                ).astype(jnp.bfloat16)
+                score = lax.dot_general(
+                    q, v_keys[b], (((1,), (1,)), ((), ())), preferred_element_type=jnp.float32
+                ) * (1.0 / math.sqrt(HD))
+                score = jnp.where(place < lengths[b], score, jnp.float32(-1e30))
+                w = jnp.exp(score - jnp.max(score, axis=1, keepdims=True))
+                probs = (w / jnp.sum(w, axis=1, keepdims=True)).astype(jnp.bfloat16)
+                o = jnp.dot(probs, v_values[b], preferred_element_type=jnp.float32)
+                heads_out[b] = jnp.where(low, o[:, :HD], o[:, HD:])
+            return 0
+
+        lax.fori_loop(0, half // TOGETHER, some, 0)
+        rows = pl.ds(h * half, half)
+        for i in range(HQ):
+            rows_one[me, rows, i * HD : (i + 1) * HD] = heads_out[rows, i, :].astype(jnp.bfloat16)
+
+    attend_half(0)
     pl.semaphore_wait(barrier, n - 1)
 
     def order(j):
@@ -137,7 +179,7 @@
         sign = jnp.where(both, jnp.where(j % 2 == 1, -1, 1), rising)
         return z + sign * dist
 
-    def gather(buf, send, recv, use):
+    def gather(buf, send, recv, use, prepare=None):
         def copy(b, h, way, target):
             piece = buf.at[b, pl.ds(h * half, half), :]
             return remote(piece, piece, send.at[b, h, way], recv.at[b, h], target)
@@ -165,6 +207,12 @@
                     @pl.when(j > 0)
                     def _():
                         copy(b, h, SIBLING, sib).wait_recv()
+
+                    if prepare is not None and h > 0:
+
+                        @pl.when(j == 0)
+                        def _():
+                            prepare(h)
 
                     sends(zj, b, h, lambda c: c.start())
 
@@ -227,7 +275,7 @@
             def _():
                 col_copy(b, me).start()
 
-    drain_one = gather(rows_one, send_one, recv_one, project)
+    drain_one = gather(rows_one, send_one, recv_one, project, attend_half)
     arrived[me] = cols[me]
 
     def take(i, _):
@@ -466,20 +514,20 @@
     t_dev, model = residual.shape
     width = out_weight.shape[1]
     ff = w_gate.shape[2]
-    attended = attend(queries, keys, values, lengths)
-    experts = jnp.arange(n, dtype=jnp.int32)
-    named = expert_ids[None, :, :] == experts[:, None, None]
-    share = jnp.sum(jnp.where(named, routed_gate_weight[None], 0.0), axis=2)
-    share = jnp.zeros((n, 8, 128), jnp.float32).at[:, 0, :t_dev].set(share)
     vmem, anywhere = pl.BlockSpec(memory_space=pltpu.VMEM), pl.BlockSpec(memory_space=pl.ANY)
     b16, f32 = jnp.bfloat16, jnp.float32
     dma = pltpu.SemaphoreType.DMA
     return pl.pallas_call(
         functools.partial(layer_kernel, n),
         out_shape=jax.ShapeDtypeStruct((t_dev, model), b16),
-        in_specs=[vmem] * 4 + [anywhere] * 4,
+        in_specs=[pl.BlockSpec(memory_space=pltpu.SMEM)] + [vmem] * 5 + [anywhere] * 6,
         out_specs=vmem,
         scratch_shapes=[
+            pltpu.VMEM((t_dev, HQ, HD), f32),
+            pltpu.VMEM((t_dev, HQ, HD), f32),
+            pltpu.VMEM(keys.shape, b16),
+            pltpu.VMEM(values.shape, b16),
+            pltpu.VMEM((n, 8, 128), f32),
             pltpu.VMEM((n, t_dev, model), b16),
             pltpu.VMEM((n, t_dev, model), b16),
             pltpu.VMEM((n, t_dev, width), b16),
@@ -497,6 +545,7 @@
             pltpu.VMEM((model, ff), b16),
             pltpu.VMEM((ff, model), b16),
             dma((4,)),
+            dma((HALVES, 2)),
             dma((n, HALVES, 4)),
             dma((n, HALVES)),
             dma((n, HALVES, 4)),
@@ -515,13 +564,17 @@
             dma((depth, HALVES)),
         ],
         compiler_params=pltpu.CompilerParams(
-            collective_id=0, has_side_effects=True, vmem_limit_bytes=62 * 1024 * 1024
+            collective_id=0, has_side_effects=True, vmem_limit_bytes=63 * 1024 * 1024
         ),
     )(
-        attended,
+        lengths,
+        queries,
         residual,
         norm_gain.reshape(1, model),
-        share,
+        expert_ids,
+        routed_gate_weight,
+        keys,
+        values,
         out_weight,
         w_gate[0],
         w_up[0],

time: 117 us -> 120 us (1.026)
  Pallas kernels: 104 us -> 114 us
  matrix products: 6.39 us -> 0 us
    pallas_call x1, Pallas kernels: 104 us -> 114 us  [per_device(): pl.pallas_call(functools.partial(layer_kernel, n), out_shape=jax.ShapeDty...]
    sub x1 -> x0, matrix products: 4.32 us -> none  [attend(): weights = jnp.exp(scores - highest)]
    dot_general x1 -> x0, matrix products: 2.08 us -> none  [attend(): jnp.einsum('bgqp,bpgd->bgqd', probs, value_heads, preferred_element_type=...]
    unnamed x11 -> x3, local copies, waits for them, and re-layouts: 3.66 us -> 4.38 us
where the time goes in v4:
time: 120 us; the launch traced here: 119 us
  Pallas kernels  114 us (95%)
  local copies, waits for them, and re-layouts  5.7 us (5%)
    pallas_call x1, Pallas kernels, per_device(): pl.pallas_call(functools.partial(layer_kernel, n), out_shape=jax.ShapeDty...  114 us
    unnamed x3, local copies, waits for them, and re-layouts  4.38 us

profile of v4, /device:TPU:1, one launch (start us, length us, event | category | flops | bytes accessed | tf_op | source)
XLA Modules:
  0.0 119.2 jit_solution(8728646262524708176)
XLA Ops:
  0.0 1.3 %reshape.3.gain = bf16[1,4096]{1,0:T(2,128)(2,1)} reshape(bf16[4096]{0:T(1024)(128)(2,1)} %param.18) | data formatting | bytes 16384 | tf_op jit(solution)/shard_map/reshape | solution.py:573
  1.3 1.4 %copy.13.ids = s32[32,8]{1,0:T(8,128)} copy(s32[32,8]{0,1:T(8,128)} %param.19) | data formatting | bytes 2048 | tf_op args[7]
  2.7 1.4 %copy.14.routed = f32[32,8]{1,0:T(8,128)} copy(f32[32,8]{0,1:T(8,128)} %param.20) | data formatting | bytes 2048 | tf_op args[8]
  4.0 113.5 %shard_map.118 = bf16[32,4096]{1,0:T(8,128)(2,1)} custom-call(s32[32]{0:T(128)} %lengths.1, bf16[32,4096]{1,0:T(8,128)(2,1)} %queries.1, bf16[32,4096]{1,0:T(8,128)(2,1)} %residual.1, bf16[1,4096]{1,0:T(2,128)(2,1)} %reshape.3.gain, s32[32,8]{1,0:T(8,128)} %copy.13.ids, f32[32,8]{1,0:T(8,128)} %copy.14.routed, bf16[32,160,256]{2,1,0:T(8,128)(2,1)} %keys.1, ...), custom_call_target="tpu_custom_call" | custom-call | tf_op jit(solution)/shard_map/pallas_call | solution.py:520
  117.6 1.7 %copy.16 = bf16[32,4096]{1,0:T(8,128)(2,1)} copy(bf16[32,4096]{1,0:T(8,128)(2,1)} %shard_map.118) | data formatting | bytes 524288

commit v5 on v4

--- a/solution.py
+++ b/solution.py
@@ -15,7 +15,7 @@
 
 MESH = pl.DeviceIdType.MESH
 HALVES = 2
-TOGETHER = 8
+TOGETHER = 16
 UP, DOWN, ACROSS, SIBLING = 0, 1, 2, 3
 
 
@@ -129,13 +129,10 @@
 
     lax.fori_loop(1, n, greet, 0)
 
-    expert_lane = lax.broadcasted_iota(jnp.int32, (t_dev, 128), 1)
-    dense = jnp.zeros((t_dev, 128), jnp.float32)
-    for i in range(ids.shape[1]):
-        dense += jnp.where(ids[:, i : i + 1] == expert_lane, routed[:, i : i + 1], 0.0)
-    turned = jnp.concatenate([dense, jnp.zeros((128 - t_dev, 128), jnp.float32)], axis=0).T
+    empty = jnp.zeros((8, 128 - t_dev), jnp.float32)
     for e in range(n):
-        share[e] = jnp.broadcast_to(turned[e : e + 1, :], (8, 128))
+        row = jnp.sum(jnp.where(ids[...] == e, routed[...], 0.0), axis=0, keepdims=True)
+        share[e] = jnp.concatenate([jnp.broadcast_to(row, (8, t_dev)), empty], axis=1)
 
     for i in range(HQ):
         heads_in[:, i, :] = queries[:, i * HD : (i + 1) * HD].astype(jnp.float32)
@@ -292,10 +289,11 @@
         stream[:, cut] = piece
         squares += piece * piece
     scale = lax.rsqrt(jnp.sum(squares, axis=1, keepdims=True) * (1.0 / model) + 1e-06)
+    gains = gain[...].astype(jnp.float32).reshape(1, model)
     for s in range(n):
         cut = pl.ds(s * width, width)
         rows_two[me, :, cut] = (
-            stream[:, cut] * scale * gain[:, cut].astype(jnp.float32)
+            stream[:, cut] * scale * gains[:, s * width : (s + 1) * width]
         ).astype(jnp.bfloat16)
     for load in loads[1:]:
         load.wait()
@@ -570,9 +568,9 @@
         lengths,
         queries,
         residual,
-        norm_gain.reshape(1, model),
-        expert_ids,
-        routed_gate_weight,
+        norm_gain,
+        expert_ids.T,
+        routed_gate_weight.T,
         keys,
         values,
         out_weight,

time: 120 us -> 115 us (0.958)
  local copies, waits for them, and re-layouts: 5.7 us -> 1.67 us
    unnamed x3 -> x1, local copies, waits for them, and re-layouts: 4.38 us -> 1.67 us
    reshape x1 -> x0, local copies, waits for them, and re-layouts: 1.31 us -> none  [per_device(): norm_gain.reshape(1, model)]
where the time goes in v5:
time: 115 us; the launch traced here: 114 us
  Pallas kernels  113 us (98%)
  local copies, waits for them, and re-layouts  1.67 us (1%)
    pallas_call x1, Pallas kernels, per_device(): pl.pallas_call(functools.partial(layer_kernel, n), out_shape=jax.ShapeDty...  113 us

profile of v5, /device:TPU:1, one launch (start us, length us, event | category | flops | bytes accessed | tf_op | source)
XLA Modules:
  0.0 114.4 jit_solution(7603978863699565736)
XLA Ops:
  0.0 112.8 %shard_map.118 = bf16[32,4096]{1,0:T(8,128)(2,1)} custom-call(s32[32]{0:T(128)} %lengths.1, bf16[32,4096]{1,0:T(8,128)(2,1)} %queries.1, bf16[32,4096]{1,0:T(8,128)(2,1)} %residual.1, bf16[4096]{0:T(1024)(128)(2,1)} %gain.1, s32[8,32]{1,0:T(8,128)} %bitcast.8, f32[8,32]{1,0:T(8,128)} %bitcast.9, bf16[32,160,256]{2,1,0:T(8,128)(2,1)} %keys.1, ...), custom_call_target="tpu_custom_call" | custom-call | tf_op jit(solution)/shard_map/pallas_call | solution.py:518
  112.8 1.7 %copy.14 = bf16[32,4096]{1,0:T(8,128)(2,1)} copy(bf16[32,4096]{1,0:T(8,128)(2,1)} %shard_map.118) | data formatting | bytes 524288
